TPU v7x, 32 devices: a whole 2x2x4 slice. The times are simulated.
32 devices in a mesh: seq: 16 (over z, x, core), tp: 2 (over y).
Axes of the slice: x: 2, y: 2, z: 4, core: 2. Of those that a mesh axis runs over, the one named last changes fastest.
Arguments:
- layer_input: bfloat16 [4608, 896], P('seq'), may hold values from -6 to 6
- block_order: int32 [32], replicated, may hold values from 0 to 31, each once
- attn_gain: float32 [896], replicated, may hold values from 0.5 to 1.5
- query_weight: bfloat16 [896, 896], P(None, 'tp'), may hold values from -0.1875 to 0.1875
- query_bias: float32 [896], P('tp'), may hold values from -3 to 3
- key_weight: bfloat16 [896, 128], P(None, 'tp'), may hold values from -0.1875 to 0.1875
- key_bias: float32 [128], P('tp'), may hold values from -3 to 3
- value_weight: bfloat16 [896, 128], P(None, 'tp'), may hold values from -0.1875 to 0.1875
- value_bias: float32 [128], P('tp'), may hold values from -1.2 to 1.2
- out_weight: bfloat16 [896, 896], P('tp'), may hold values from -1.5 to 1.5
- mlp_gain: float32 [896], replicated, may hold values from 0.5 to 1.5
- gate_weight: bfloat16 [896, 4864], P(None, 'tp'), may hold values from -0.1875 to 0.1875
- up_weight: bfloat16 [896, 4864], P(None, 'tp'), may hold values from -0.1875 to 0.1875
- down_weight: bfloat16 [4864, 896], P('tp'), may hold values from -0.078125 to 0.078125
- out_cotangent: bfloat16 [4608, 896], P('seq'), may hold values from -6 to 6
Outputs:
- layer_output: bfloat16 [4608, 896], P('seq')
- input_grad: bfloat16 [4608, 896], P('seq')
- attn_gain_grad: float32 [896], replicated
- query_weight_grad: float32 [896, 896], P(None, 'tp')
- query_bias_grad: float32 [896], P('tp')
- key_weight_grad: float32 [896, 128], P(None, 'tp')
- key_bias_grad: float32 [128], P('tp')
- value_weight_grad: float32 [896, 128], P(None, 'tp')
- value_bias_grad: float32 [128], P('tp')
- out_weight_grad: float32 [896, 896], P('tp')
- mlp_gain_grad: float32 [896], replicated
- gate_weight_grad: float32 [896, 4864], P(None, 'tp')
- up_weight_grad: float32 [896, 4864], P(None, 'tp')
- down_weight_grad: float32 [4864, 896], P('tp')
Inputs may be any that keep to these rules, and one draw needn't show every extreme that they name: `block_order`: A permutation: each of the 32 blocks of 144 consecutive positions stands in exactly one slot.
All inputs are finite; a program needn't handle non-finite values.
Results may differ from a plain program's by a relative error of at most 0.03.
Values may be sent and summed in bfloat16 or wider, within the bound.
A program may use at most 192 MiB of HBM per device.

v0:
```python
import functools

import jax
import jax.numpy as jnp
from jax import lax
from jax.experimental import pallas as pl
from jax.experimental.pallas import tpu as pltpu
from jax.sharding import PartitionSpec as P

HEAD_DIM = 64
EPSILON = 1e-06
NEGATIVE = -1e30
ROPE_BASE = 1000000.0
LANES = 128
QUAD = 4
WIDE_ROWS = 128
TALL_ROWS = 64
SHARE = (2, 2, 2, 2, 1, 1, 1, 2, 1, 1, 2, 1, 1, 1, 1)
PACE = 2
MESH = pl.DeviceIdType.MESH
VMEM_LIMIT = 62 * 1024 * 1024
BF16 = jnp.bfloat16
F32 = jnp.float32


def round_up(value, step):
    return -(-value // step) * step


def nn(left, right):
    return lax.dot_general(left, right, (((1,), (0,)), ((), ())), preferred_element_type=F32)


def nt(left, right):
    return lax.dot_general(left, right, (((1,), (1,)), ((), ())), preferred_element_type=F32)


def tn(left, right):
    return lax.dot_general(left, right, (((0,), (0,)), ((), ())), preferred_element_type=F32)


class Place:
    def __init__(self, groups):
        seq = lax.axis_index("seq").astype(jnp.int32)
        tp = lax.axis_index("tp").astype(jnp.int32)
        self.groups = groups
        self.seq = seq
        self.tp = tp
        self.group = seq // QUAD
        self.quad = seq % QUAD
        self.core = seq % 2
        self.side = (seq // 2) % 2
        self.sibling = (seq + 1 - 2 * self.core, tp)
        self.across = (seq + 2 - 4 * self.side, tp)
        self.partner = (seq, 1 - tp)

    def seq_at(self, group, side, core):
        return group * QUAD + side * 2 + core

    def in_group(self, group):
        return (group * QUAD + self.quad, self.tp)


def send(src, dst, send_sem, recv_sem, device):
    pltpu.make_async_remote_copy(
        src_ref=src,
        dst_ref=dst,
        send_sem=send_sem,
        recv_sem=recv_sem,
        device_id=device,
        device_id_type=MESH,
    ).start()


def sent(src, send_sem, device):
    pltpu.make_async_remote_copy(
        src_ref=src,
        dst_ref=src,
        send_sem=send_sem,
        recv_sem=send_sem,
        device_id=device,
        device_id_type=MESH,
    ).wait_send()


def arrived(dst, recv_sem, device):
    pltpu.make_async_remote_copy(
        src_ref=dst,
        dst_ref=dst,
        send_sem=recv_sem,
        recv_sem=recv_sem,
        device_id=device,
        device_id_type=MESH,
    ).wait_recv()


def meet(place, whole_column):
    barrier = pltpu.get_barrier_semaphore()
    for device in (place.sibling, place.across, place.partner):
        pl.semaphore_signal(barrier, inc=1, device_id=device, device_id_type=MESH)
    if whole_column:
        for step in range(1, place.groups):
            other = place.in_group((place.group + step) % place.groups)
            pl.semaphore_signal(barrier, inc=1, device_id=other, device_id_type=MESH)
        pl.semaphore_wait(barrier, 3 + place.groups - 1)
    else:
        pl.semaphore_wait(barrier, 3)


class LayerGather:
    def __init__(self, place, all_ref, half, recv, part, sems):
        self.place = place
        self.all_ref = all_ref
        self.half = half
        self.first = round_up(half // 2, 16)
        self.recv, self.part, self.sems = recv, part, sems

    def index(self, flip_side, flip_core, flip_tp):
        place = self.place
        side = 1 - place.side if flip_side else place.side
        core = 1 - place.core if flip_core else place.core
        tp = 1 - place.tp if flip_tp else place.tp
        return (side * 2 + core) * 2 + tp

    def rows(self, block, start=0, size=None):
        size = self.half if size is None else size
        return self.all_ref.at[pl.ds(pl.multiple_of(block * self.half + start, 16), size)]

    def start(self, numbers=(0, 1, 2)):
        place = self.place
        own = self.index(0, 0, 0)
        devices = (place.across, place.partner, place.sibling)
        for number in numbers:
            send(
                self.rows(own),
                self.rows(own),
                self.sems.at[number],
                self.recv.at[own],
                devices[number],
            )

    def from_across(self):
        place = self.place
        block = self.index(1, 0, 0)
        arrived(self.rows(block), self.recv.at[block], place.across)
        part = self.rows(block, 0, self.first)
        send(part, part, self.sems.at[3], self.part.at[0], place.partner)
        send(self.rows(block), self.rows(block), self.sems.at[4], self.recv.at[block], place.sibling)

    def from_partner(self):
        place = self.place
        block = self.index(0, 0, 1)
        arrived(self.rows(block), self.recv.at[block], place.partner)
        part = self.rows(block, self.first, self.half - self.first)
        send(part, part, self.sems.at[5], self.part.at[1], place.across)
        send(self.rows(block), self.rows(block), self.sems.at[6], self.recv.at[block], place.sibling)

    def diagonal(self):
        place = self.place
        block = self.index(1, 0, 1)
        arrived(self.rows(block, 0, self.first), self.part.at[0], place.partner)
        arrived(self.rows(block, self.first, self.half - self.first), self.part.at[1], place.across)
        send(self.rows(block), self.rows(block), self.sems.at[7], self.recv.at[block], place.sibling)

    def from_sibling(self, flip_side, flip_tp):
        block = self.index(flip_side, 1, flip_tp)
        arrived(self.rows(block), self.recv.at[block], self.place.sibling)

    def finish(self, waited=False):
        place = self.place
        if not waited:
            for side in (0, 1):
                for tp in (0, 1):
                    self.from_sibling(side, tp)
        own = self.index(0, 0, 0)
        for number, device in enumerate((place.across, place.partner, place.sibling)):
            sent(self.rows(own), self.sems.at[number], device)
        sent(self.rows(own, 0, self.first), self.sems.at[3], place.partner)
        sent(self.rows(own), self.sems.at[4], place.sibling)
        sent(self.rows(own, self.first, self.half - self.first), self.sems.at[5], place.across)
        sent(self.rows(own), self.sems.at[6], place.sibling)
        sent(self.rows(own), self.sems.at[7], place.sibling)


def extended_keys(kv, chip, rows, width, slots):
    count = kv.shape[0]
    lane = lax.broadcasted_iota(jnp.int32, (count, width), 1) - HEAD_DIM
    row = lax.broadcasted_iota(jnp.int32, (count, width), 0)
    block = rows // 2
    number = jnp.zeros_like(row)
    for edge in range(block, count, block):
        number = number + (row >= edge).astype(jnp.int32)
    hot = (lane == number + chip * (count // block)) | ((lane >= slots) & (lane < slots + 3))
    extra = jnp.where(hot, 1.0, 0.0).astype(BF16)
    if width == LANES:
        return jnp.where(lane < 0, kv, extra)
    first = jnp.where(lane[:, :LANES] < 0, kv, extra[:, :LANES])
    return jnp.concatenate([first, extra[:, LANES:]], axis=1)


def hide_later(scores, place, rows, half_number, first):
    count, width = scores.shape
    half = rows // 2
    key = lax.broadcasted_iota(jnp.int32, (count, 1), 0) - place.core * rows - half_number * half
    query = (lax.broadcasted_iota(jnp.int32, (1, width), 1) + first) % half
    return jnp.where((key > query) & (key < half), NEGATIVE, scores)


def split_rows(values, at, count):
    one = values.astype(BF16).astype(F32)
    two = (values - one).astype(BF16).astype(F32)
    three = values - one - two
    row = lax.broadcasted_iota(jnp.int32, (count, values.shape[1]), 0) - at
    picked = jnp.where(row == 0, one, jnp.where(row == 1, two, jnp.where(row == 2, three, 0.0)))
    return picked.astype(BF16)


def attend_kernel(
    groups,
    slots,
    kv_own,
    qt,
    x_in,
    out_weight,
    cot,
    kv_all,
    cot_all,
    resid_out,
    att_out,
    ot_out,
    lse_out,
    s_buf,
    m_buf,
    l_buf,
    part_send,
    part_recv,
    kv_recv,
    kv_z,
    kv_x,
    kv_sib,
    c_recv,
    c_part,
    c_sems,
    p_sems,
):
    place = Place(groups)
    rows = kv_own.shape[0]
    half = rows // 2
    span = 2 * rows
    width, queries = qt.shape
    block = queries // 2
    chunks = 2 * groups
    heads = out_weight.shape[0] // HEAD_DIM

    kv_all[pl.ds(place.seq * rows, rows), :] = kv_own[...]
    own_half = place.quad * 2 + place.tp
    cot_all[pl.ds(pl.multiple_of(own_half * half, 16), half), :] = cot[
        pl.ds(pl.multiple_of(place.tp * half, 16), half), :
    ]
    meet(place, True)

    def kv_rows(seq):
        return kv_all.at[pl.ds(pl.multiple_of(seq * rows, 16), rows)]

    gather_cot = LayerGather(place, cot_all, half, c_recv, c_part, c_sems)
    own = kv_rows(place.seq)
    send(own, own, kv_sib.at[0], kv_recv.at[place.seq], place.sibling)
    for step in range(1, groups):
        other = place.in_group((place.group + step) % groups)
        send(own, own, kv_z.at[step - 1], kv_recv.at[place.seq], other)
    send(own, own, kv_x.at[0], kv_recv.at[place.seq], place.across)
    gather_cot.start((1, 2))

    def chunk_place(number):
        odd = number % 2
        far = jnp.where(number < 2, odd, jnp.where(number == 2, 0, 1 - odd))
        distance = jnp.where(number < 2, 0, jnp.where(odd == 1, (number + 1) // 2, number // 2 - 1))
        distance = jnp.where(number == 2, 1, distance)
        last = number == chunks - 1
        far = jnp.where(last, 1, far)
        distance = jnp.where(last, groups - 1, distance)
        up = jnp.where(place.group < groups // 2, distance, groups - distance)
        group = (place.group + up) % groups
        side = place.side + far * (1 - 2 * place.side)
        return group, side, distance, far

    def pass_on(number):
        group, side, distance, far = chunk_place(number)
        seq = place.seq_at(group, side, place.core)
        view = kv_rows(seq)
        arrived(view, kv_recv.at[seq], place.across)
        send(view, view, kv_sib.at[number], kv_recv.at[seq], place.sibling)

        @pl.when(far == 0)
        def near():
            send(view, view, kv_x.at[distance], kv_recv.at[seq], place.across)

    def ready(number):
        group, side, _, _ = chunk_place(number)
        seq = place.seq_at(group, side, 1 - place.core)
        arrived(kv_rows(seq), kv_recv.at[seq], place.sibling)

    def kv_chunk(number):
        group, side, _, _ = chunk_place(number)
        chip = group * 2 + side
        return chip, kv_all[pl.ds(pl.multiple_of(chip * span, 16), span), :]

    def lanes_of(half_number):
        return pl.ds(pl.multiple_of(half_number * block, LANES), block)

    def scores(half_number, number, slot, own_chip=False):
        chip, kv = kv_chunk(number)
        keys = extended_keys(kv, chip, rows, width, slots)
        value = nn(keys, qt[:, lanes_of(half_number)])
        if own_chip:
            value = hide_later(value, place, rows, half_number, 0)
        s_buf[slot] = value

    def absorb(half_number, number, slot):
        chip, kv = kv_chunk(number)
        lanes = lanes_of(half_number)
        value = s_buf[slot]
        old = m_buf[:, lanes]
        top = jnp.maximum(old, jnp.max(value, axis=0, keepdims=True))
        shrink = jnp.exp(old - top)
        weights = jnp.exp(value - top)
        total = jnp.sum(weights, axis=0, keepdims=True)
        product = tn(kv[:, HEAD_DIM:], weights.astype(BF16))
        m_buf[:, lanes] = top
        l_buf[:, lanes] = total + l_buf[:, lanes] * shrink
        ot_out[:, lanes] = product + ot_out[:, lanes] * shrink

    m_buf[...] = jnp.full(m_buf.shape, NEGATIVE, F32)
    l_buf[...] = jnp.zeros_like(l_buf)
    ot_out[...] = jnp.zeros_like(ot_out)

    def comes(number):
        @pl.when(number + 2 < chunks)
        def look_ahead():
            pass_on(number + 2)

        @pl.when(number < chunks)
        def next_ready():
            ready(number)

    def sweep(half_number, waits, following):
        def two_chunks(pair, unused):
            if waits:
                comes(2 * pair + 1)
            scores(half_number, 2 * pair + 1, 1)
            absorb(half_number, 2 * pair, 0)
            if waits:
                comes(2 * pair + 2)
            scores(half_number, 2 * pair + 2, 0)
            absorb(half_number, 2 * pair + 1, 1)
            return unused

        lax.fori_loop(0, groups - 1, two_chunks, 0)
        if waits:
            comes(chunks - 1)
        scores(half_number, chunks - 1, 1)
        absorb(half_number, chunks - 2, 0)
        if following is not None:
            scores(following, 0, 0, True)
        absorb(half_number, chunks - 1, 1)

    def close_half(half_number):
        lanes = lanes_of(half_number)
        ot = ot_out[:, lanes] / l_buf[:, lanes]
        ot_out[:, lanes] = ot
        lse_out[:, lanes] = m_buf[:, lanes] + jnp.log(l_buf[:, lanes])
        natural = jnp.transpose(ot).astype(BF16)
        att = jnp.concatenate(
            [natural[head * half : (head + 1) * half, :] for head in range(heads)], axis=1
        )
        att_out[pl.ds(pl.multiple_of(half_number * half, 16), half), :] = att
        return nn(att, out_weight[...])

    theirs, mine = 1 - place.tp, place.tp
    ready(0)
    scores(theirs, 0, 0, True)
    pass_on(1)
    pass_on(2)
    sweep(theirs, True, mine)
    gather_cot.start((0,))
    part_send[...] = close_half(theirs).astype(BF16)
    send(part_send, part_recv, p_sems.at[0], p_sems.at[1], place.partner)
    gather_cot.from_partner()
    sweep(mine, False, None)
    gather_cot.from_across()
    my_rows = pl.ds(pl.multiple_of(place.tp * half, 16), half)
    resid = close_half(mine) + x_in[my_rows, :].astype(F32)
    gather_cot.diagonal()
    arrived(part_recv, p_sems.at[1], place.partner)
    resid_out[...] = resid + part_recv[...].astype(F32)
    gather_cot.finish()
    sent(part_send, p_sems.at[0], place.partner)

    def close(number, unused):
        sent(own, kv_sib.at[number], place.sibling)
        return unused

    lax.fori_loop(0, chunks, close, 0)
    for step_out in range(groups):
        sent(own, kv_x.at[step_out], place.across)
    for step_out in range(1, groups):
        sent(own, kv_z.at[step_out - 1], place.in_group((place.group + step_out) % groups))


class ChainSum:
    def __init__(self, place, own, incoming, at_root, final, sems):
        self.place = place
        self.own, self.incoming, self.at_root, self.final = own, incoming, at_root, final
        self.count = own.shape[0]
        (
            self.up_recv,
            self.up_send,
            self.fin_recv,
            self.fin_send,
            self.x_recv,
            self.x_send,
            self.c_recv,
            self.c_send,
            self.keep,
        ) = sems

    def root(self, parity):
        return self.place.groups // 2 - 1 + parity

    def lag_up(self, parity):
        groups, group, root = self.place.groups, self.place.group, self.root(parity)
        most = max(root, groups - 1 - root)
        return PACE * jnp.where(
            group < root, group, jnp.where(group > root, groups - 1 - group, most)
        )

    def lag_down(self, parity):
        groups, group, root = self.place.groups, self.place.group, self.root(parity)
        most = max(root, groups - 1 - root)
        return PACE * (most + jnp.abs(group - root))

    def total_steps(self):
        groups = self.place.groups
        most = groups // 2
        return self.count + PACE * (2 * most + 1)

    def spread(self, i, view):
        place = self.place
        final = self.final.at[place.quad, i]
        send(view, final, self.x_send.at[i], self.x_recv.at[i], place.across)
        send(view, final, self.c_send.at[0, i], self.c_recv.at[0, i], place.sibling)

    def up(self, i, parity):
        place, root = self.place, self.root(parity)
        group, last = place.group, place.groups - 1
        mine = self.own.at[i]

        here, second = self.incoming.at[i], self.at_root.at[i // 2]

        def add(way, ref):
            arrived(ref, self.up_recv.at[way, i], place.in_group(group - 1 + 2 * way))
            mine[...] = (mine[...].astype(F32) + ref[...].astype(F32)).astype(BF16)

        def onward(way, dst, send_sem, recv_sem):
            send(mine, dst, send_sem, recv_sem, place.in_group(group + 1 - 2 * way))

        @pl.when((group > 0) & (group <= root))
        def from_left():
            add(0, here)

        @pl.when((group < last) & (group > root))
        def from_right():
            add(1, here)

        @pl.when((group < last) & (group == root))
        def from_right_to_root():
            add(1, second)

        @pl.when(group < root)
        def to_right():
            onward(0, here, self.up_send.at[i], self.up_recv.at[0, i])

        @pl.when(group > root + 1)
        def to_left():
            onward(1, here, self.up_send.at[i], self.up_recv.at[1, i])

        @pl.when(group == root + 1)
        def to_root():
            onward(1, second, self.up_send.at[i], self.up_recv.at[1, i])

        @pl.when(group == root)
        def finished():
            final = self.final.at[place.quad, i]

            @pl.when(group > 0)
            def left():
                onward(1, final, self.fin_send.at[0, i], self.fin_recv.at[i])

            @pl.when(group < last)
            def right():
                onward(0, final, self.fin_send.at[1, i], self.fin_recv.at[i])

            self.spread(i, mine)
            pltpu.make_async_copy(mine, final, self.keep.at[i]).start()

    def down(self, i, parity):
        place, root = self.place, self.root(parity)
        group, last = place.group, place.groups - 1
        view = self.final.at[place.quad, i]

        @pl.when(group != root)
        def take():
            arrived(view, self.fin_recv.at[i], place.sibling)

            @pl.when((group < root) & (group > 0))
            def left():
                send(
                    view,
                    view,
                    self.fin_send.at[0, i],
                    self.fin_recv.at[i],
                    place.in_group(group - 1),
                )

            @pl.when((group > root) & (group < last))
            def right():
                send(
                    view,
                    view,
                    self.fin_send.at[1, i],
                    self.fin_recv.at[i],
                    place.in_group(group + 1),
                )

            self.spread(i, view)

    def cross(self, i):
        place = self.place
        view = self.final.at[place.across[0] % QUAD, i]
        arrived(view, self.x_recv.at[i], place.across)
        send(view, view, self.c_send.at[1, i], self.c_recv.at[1, i], place.sibling)

    def step(self, number):
        for parity in (0, 1):
            i = number - self.lag_up(parity)

            @pl.when((i >= 0) & (i < self.count) & (i % 2 == parity))
            def go_up(i=i, parity=parity):
                self.up(i, parity)

        for parity in (0, 1):
            i = number - self.lag_down(parity)

            @pl.when((i >= 0) & (i < self.count) & (i % 2 == parity))
            def go_down(i=i, parity=parity):
                self.down(i, parity)

        for parity in (0, 1):
            i = number - self.lag_down(parity) - PACE

            @pl.when((i >= 0) & (i < self.count) & (i % 2 == parity))
            def go_cross(i=i):
                self.cross(i)

    def finish(self):
        place = self.place
        group, last = place.group, place.groups - 1
        sibling_quad = place.sibling[0] % QUAD
        diagonal = 3 - place.quad

        def close(i, unused):
            root = place.groups // 2 - 1 + i % 2
            view = self.own.at[i]
            arrived(self.final.at[sibling_quad, i], self.c_recv.at[0, i], place.sibling)
            arrived(self.final.at[diagonal, i], self.c_recv.at[1, i], place.sibling)

            @pl.when(group != root)
            def up_done():
                sent(view, self.up_send.at[i], place.sibling)

            @pl.when(group == root)
            def kept():
                final = self.final.at[place.quad, i]
                pltpu.make_async_copy(view, final, self.keep.at[i]).wait()

            @pl.when((group <= root) & (group > 0))
            def left_done():
                sent(view, self.fin_send.at[0, i], place.sibling)

            @pl.when((group >= root) & (group < last))
            def right_done():
                sent(view, self.fin_send.at[1, i], place.sibling)

            sent(view, self.x_send.at[i], place.across)
            sent(view, self.c_send.at[0, i], place.sibling)
            sent(view, self.c_send.at[1, i], place.sibling)
            return unused

        lax.fori_loop(0, self.count, close, 0)


def chain_sems(count):
    dma = pltpu.SemaphoreType.DMA
    return [
        dma((2, count)),
        dma((count,)),
        dma((count,)),
        dma((2, count)),
        dma((count,)),
        dma((count,)),
        dma((2, count)),
        dma((2, count)),
        dma((count,)),
    ]


class LayerSum:
    def __init__(self, place, part, half, core_in, left, right, left_in, right_in, last_in, sems):
        self.place, self.part, self.half = place, part, half
        self.core_in, self.left, self.right = core_in, left, right
        self.left_in, self.right_in, self.last_in = left_in, right_in, last_in
        self.sems = sems
        self.cut = left.shape[2]
        self.columns = part.shape[1]

    def rows(self, side, core):
        size = 2 * self.half
        return pl.ds(pl.multiple_of((side * 2 + core) * size, 16), size)

    def start(self):
        place = self.place
        for side in (0, 1):
            view = self.part.at[self.rows(side, 1 - place.core)]
            send(
                view,
                self.core_in.at[side],
                self.sems.at[side],
                self.sems.at[2 + side],
                place.sibling,
            )

    def own_rows(self, tp):
        return pl.ds(pl.multiple_of(tp * self.half, 16), self.half)

    def after_core(self):
        place = self.place
        for side in (0, 1):
            arrived(self.core_in.at[side], self.sems.at[2 + side], place.sibling)
            total = self.part[self.rows(side, place.core), :].astype(F32) + self.core_in[
                side
            ].astype(F32)
            self.left[side] = total[:, : self.cut].astype(BF16)
            self.right[side] = total[:, self.cut :].astype(BF16)

    def cross(self):
        place = self.place
        for side in (0, 1):
            send(
                self.left.at[side, self.own_rows(1 - place.tp)],
                self.left_in.at[side],
                self.sems.at[4 + side],
                self.sems.at[6 + side],
                place.partner,
            )
        send(
            self.right.at[1 - place.side],
            self.right_in,
            self.sems.at[8],
            self.sems.at[9],
            place.across,
        )

    def after_cross(self):
        place = self.place
        mine = self.own_rows(place.tp)
        for side in (0, 1):
            arrived(self.left_in.at[side], self.sems.at[6 + side], place.partner)
            self.left_in[side] = (
                self.left[side, mine, :].astype(F32) + self.left_in[side].astype(F32)
            ).astype(BF16)
        arrived(self.right_in, self.sems.at[9], place.across)
        self.right_in[...] = (
            self.right[place.side].astype(F32) + self.right_in[...].astype(F32)
        ).astype(BF16)
        send(
            self.left_in.at[1 - place.side],
            self.last_in.at[:, : self.cut],
            self.sems.at[10],
            self.sems.at[11],
            place.across,
        )
        send(
            self.right_in.at[self.own_rows(1 - place.tp)],
            self.last_in.at[:, self.cut :],
            self.sems.at[12],
            self.sems.at[13],
            place.partner,
        )

    def result(self):
        place = self.place
        arrived(self.last_in.at[:, : self.cut], self.sems.at[11], place.across)
        arrived(self.last_in.at[:, self.cut :], self.sems.at[13], place.partner)
        mine = jnp.concatenate(
            [self.left_in[place.side], self.right_in[self.own_rows(place.tp), :]], axis=1
        )
        return mine.astype(F32) + self.last_in[...].astype(F32)

    def finish(self):
        place = self.place
        for side in (0, 1):
            sent(self.core_in.at[side], self.sems.at[side], place.sibling)
            sent(self.left_in.at[side], self.sems.at[4 + side], place.partner)
        sent(self.right_in, self.sems.at[8], place.across)
        sent(self.last_in.at[:, : self.cut], self.sems.at[10], place.across)
        sent(self.last_in.at[:, self.cut :], self.sems.at[12], place.partner)


class QuadSum:
    def __init__(self, place, part, own, core_in, x_send, x_in, sems):
        self.place, self.part, self.own = place, part, own
        self.core_in, self.x_send, self.x_in, self.sems = core_in, x_send, x_in, sems

    def start(self):
        place = self.place
        for side in (0, 1):
            send(
                self.part.at[side * 2 + 1 - place.core],
                self.core_in.at[side],
                self.sems.at[side],
                self.sems.at[2 + side],
                place.sibling,
            )

    def total(self, side):
        return self.part[side * 2 + self.place.core].astype(F32) + self.core_in[side].astype(F32)

    def middle(self):
        place = self.place
        for side in (0, 1):
            arrived(self.core_in.at[side], self.sems.at[2 + side], place.sibling)
        self.x_send[...] = self.total(1 - place.side).astype(BF16)
        send(self.x_send, self.x_in, self.sems.at[4], self.sems.at[5], place.across)

    def end(self):
        place = self.place
        arrived(self.x_in, self.sems.at[5], place.across)
        mine = (self.total(place.side) + self.x_in[...].astype(F32)).astype(BF16)
        count, step = self.own.shape[0], self.own.shape[1]
        for i in range(count):
            piece = mine[i * step : (i + 1) * step, :]
            if piece.shape[0]:
                self.own[i, : piece.shape[0], :] = piece
            if piece.shape[0] < step:
                left = step - piece.shape[0]
                self.own[i, piece.shape[0] :, :] = jnp.zeros((left, piece.shape[1]), BF16)

    def finish(self):
        place = self.place
        for side in (0, 1):
            sent(self.core_in.at[side], self.sems.at[side], place.sibling)
        sent(self.x_send, self.sems.at[4], place.across)


class ColumnSum:
    def __init__(self, place, own, incoming, final, sems):
        self.place, self.own, self.incoming, self.final = place, own, incoming, final
        self.rs_send, self.rs_recv, self.ag_send, self.ag_recv = (sems.at[i] for i in range(4))
        self.x_send, self.x_recv, self.c_send, self.c_recv = (sems.at[i] for i in range(4, 8))
        self.d_send, self.d_recv = (sems.at[i] for i in range(8, 10))

    def others(self):
        place = self.place
        for step in range(1, place.groups):
            yield step, (place.group + step) % place.groups

    def start(self):
        place = self.place
        for step, other in self.others():
            back = place.groups - step
            send(
                self.own.at[other],
                self.incoming.at[back],
                self.rs_send.at[step],
                self.rs_recv.at[back],
                place.in_group(other),
            )

    def spread(self, part, view):
        place = self.place
        final = self.final.at[place.quad, part]
        send(view, final, self.x_send.at[part], self.x_recv.at[part], place.across)
        send(view, final, self.c_send.at[part], self.c_recv.at[part], place.sibling)

    def middle(self):
        place = self.place
        mine = self.own.at[place.group]
        total = mine[...].astype(F32)
        for step, other in self.others():
            arrived(self.incoming.at[step], self.rs_recv.at[step], place.sibling)
            total = total + self.incoming[step].astype(F32)
        mine[...] = total.astype(BF16)
        final = self.final.at[place.quad, place.group]
        for step, other in self.others():
            send(
                mine,
                final,
                self.ag_send.at[step],
                self.ag_recv.at[place.group],
                place.in_group(other),
            )
        self.spread(place.group, mine)
        pltpu.make_async_copy(mine, final, self.ag_send.at[0]).start()

    def end(self):
        place = self.place
        for step, other in self.others():
            view = self.final.at[place.quad, other]
            arrived(view, self.ag_recv.at[other], place.sibling)
            self.spread(other, view)

    def cross(self):
        place = self.place
        quad = place.across[0] % QUAD
        for step in range(place.groups):
            part = (place.group + step) % place.groups
            view = self.final.at[quad, part]
            arrived(view, self.x_recv.at[part], place.across)
            send(view, view, self.d_send.at[part], self.d_recv.at[part], place.sibling)

    def finish(self):
        place = self.place
        view = self.own.at[0]
        for part in range(place.groups):
            arrived(view, self.c_recv.at[part], place.sibling)
            arrived(view, self.d_recv.at[part], place.sibling)
            sent(view, self.x_send.at[part], place.across)
            sent(view, self.c_send.at[part], place.sibling)
            sent(view, self.d_send.at[part], place.sibling)
        for step, other in self.others():
            sent(view, self.rs_send.at[step], place.sibling)
            sent(view, self.ag_send.at[step], place.sibling)
        final = self.final.at[place.quad, place.group]
        pltpu.make_async_copy(self.own.at[place.group], final, self.ag_send.at[0]).wait()


def column_parts(groups, rows, columns):
    return (groups, round_up(-(-rows // groups), 16), columns)


def column_sum_scratch(groups, rows, columns):
    parts = column_parts(groups, rows, columns)
    return [
        *quad_sum_scratch(rows, columns),
        pltpu.VMEM(parts, BF16),
        pltpu.VMEM(parts, BF16),
        pltpu.SemaphoreType.DMA((10, groups)),
    ]


def quad_sum_scratch(rows, columns):
    return [
        pltpu.VMEM((QUAD, rows, columns), BF16),
        pltpu.VMEM((2, rows, columns), BF16),
        pltpu.VMEM((rows, columns), BF16),
        pltpu.VMEM((rows, columns), BF16),
        pltpu.SemaphoreType.DMA((6,)),
    ]


def layer_sum_scratch(half, columns):
    cut = columns // LANES // 2 * LANES
    if cut * 2 < columns:
        cut += LANES
    return [
        pltpu.VMEM((2, 2 * half, columns), BF16),
        pltpu.VMEM((2, 2 * half, cut), BF16),
        pltpu.VMEM((2, 2 * half, columns - cut), BF16),
        pltpu.VMEM((2, half, cut), BF16),
        pltpu.VMEM((2 * half, columns - cut), BF16),
        pltpu.VMEM((half, columns), BF16),
        pltpu.SemaphoreType.DMA((14,)),
    ]


def backward_kernel(
    groups,
    slots,
    gate_weight,
    up_weight,
    down_weight,
    cot_all,
    resid_in,
    cot,
    gain,
    out_weight,
    att,
    ot,
    lse,
    qt_in,
    kv_all,
    x_in,
    attn_gain,
    weights_in,
    turns,
    turns_rows,
    layer_out,
    input_grad,
    wide,
    tall,
    outs,
    ins_q,
    ins_kv,
    gains,
    biases,
    *scratch,
):
    place = Place(groups)
    wide_own, tall_own, wide_up, tall_up = scratch[0:4]
    wide_root, tall_root = scratch[4:6]
    scratch = scratch[2:]
    wide_sems, tall_sems = scratch[4:13], scratch[13:22]
    sum_g, sum_m = scratch[22:29], scratch[29:36]
    branch, qt, dot_t, q_pad, do_pad, dkv = scratch[36:42]
    sib_send, sib_in, side_send, side_in, z_send, z_in = scratch[42:48]
    kv_sems, pair_sems = scratch[48:50]
    dq_out, dkv_out, resid_grad = scratch[50:53]
    turn_send, turn_in, gain_in, bias_in, gain_z, bias_z, vector_sems = scratch[53:60]
    sum_o, sum_q, sum_kv = scratch[60:68], scratch[68:76], scratch[76:84]
    rows = att.shape[0]
    half = rows // 2
    span = 2 * rows
    width, queries = qt_in.shape
    parts = 2 if groups <= 4 else 8
    block = queries // parts
    chunks = 2 * groups
    heads = out_weight.shape[0] // HEAD_DIM
    my_rows = pl.ds(pl.multiple_of(place.tp * half, 16), half)
    other_rows = pl.ds(pl.multiple_of((1 - place.tp) * half, 16), half)

    tall_sum = ChainSum(place, tall_own, tall_up, tall_root, tall, tall_sems)
    wide_sum = ChainSum(place, wide_own, wide_up, wide_root, wide, wide_sems)
    gate_piece, up_piece, down_piece, normed_all, mixed, grad_gu, grad_part, mlp_part = scratch[84:92]
    gather_sems = scratch[92:95]
    features = resid_in.shape[1]
    piece = gate_piece.shape[1]
    keep = gate_weight.shape[1] - (QUAD - 1) * piece

    def load_weights(size, quad):
        columns = pl.ds(pl.multiple_of(quad * piece, LANES), size)
        pairs = (
            (gate_weight.at[:, columns], gate_piece.at[:, pl.ds(0, size)]),
            (up_weight.at[:, columns], up_piece.at[:, pl.ds(0, size)]),
            (down_weight.at[columns], down_piece.at[pl.ds(0, size)]),
        )
        return [
            pltpu.make_async_copy(src, dst, pair_sems.at[4 + number])
            for number, (src, dst) in enumerate(pairs)
        ]

    last_quad = QUAD - 1

    @pl.when(place.quad < last_quad)
    def whole_piece():
        for copy in load_weights(piece, place.quad):
            copy.start()

    @pl.when(place.quad == last_quad)
    def last_piece():
        for copy in load_weights(keep, last_quad):
            copy.start()
        if keep < piece:
            gate_piece[:, keep:] = jnp.zeros((features, piece - keep), BF16)
            up_piece[:, keep:] = jnp.zeros((features, piece - keep), BF16)
            down_piece[keep:, :] = jnp.zeros((piece - keep, features), BF16)

    grad_sum = LayerSum(place, grad_part, half, *sum_g)
    mlp_sum = LayerSum(place, mlp_part, half, *sum_m)

    def quad_and_column(final, refs):
        quad = QuadSum(place, refs[0], refs[5], *refs[1:5])
        return quad, ColumnSum(place, refs[5], refs[6], final, refs[7])

    outs_quad, outs_sum = quad_and_column(outs, sum_o)
    q_quad, q_sum = quad_and_column(ins_q, sum_q)
    kv_quad, kv_sum = quad_and_column(ins_kv, sum_kv)
    tall_steps = tall_sum.count

    def chain_step(number):
        tall_sum.step(number)
        wide_sum.step(number - tall_steps)

    def chain_steps(first, count):
        def one(number, unused):
            chain_step(number)
            return unused

        lax.fori_loop(first, first + count, one, 0)
        return first + count

    all_steps = tall_steps + wide_sum.total_steps()

    gather = LayerGather(place, normed_all, half, *gather_sems)
    resid = resid_in[...]
    factor = lax.rsqrt(jnp.mean(resid * resid, axis=-1, keepdims=True) + EPSILON)
    own_block = place.quad * 2 + place.tp
    normed_all[pl.ds(pl.multiple_of(own_block * half, 16), half), :] = (
        resid * factor * gain[...]
    ).astype(BF16)
    meet(place, True)
    gather.start()

    @pl.when(place.quad < last_quad)
    def whole_loaded():
        for copy in load_weights(piece, place.quad):
            copy.wait()

    @pl.when(place.quad == last_quad)
    def last_loaded():
        for copy in load_weights(keep, last_quad):
            copy.wait()

    def feed(number, unused):
        @pl.when(number == 1)
        def second():
            gather.from_sibling(0, 0)

        @pl.when(number == 2)
        def third():
            gather.from_partner()
            gather.from_across()

        @pl.when(number == 4)
        def fifth():
            gather.from_sibling(0, 1)

        @pl.when(number == 5)
        def sixth():
            gather.from_sibling(1, 0)
            gather.diagonal()

        @pl.when(number == 7)
        def eighth():
            gather.from_sibling(1, 1)

        def flip(value, numbers):
            turned = functools.reduce(lambda x, y: x | y, [number == i for i in numbers])
            return jnp.where(turned, 1 - value, value)

        side = flip(place.side, (3, 5, 6, 7))
        core = flip(place.core, (1, 4, 5, 7))
        tp = flip(place.tp, (2, 4, 6, 7))
        at_rows = pl.ds(pl.multiple_of(((side * 2 + core) * 2 + tp) * half, 16), half)
        here = normed_all[at_rows, :]
        gate = nn(here, gate_piece[...])
        upward = nn(here, up_piece[...])
        sigmoid = jax.nn.sigmoid(gate)
        silu = gate * sigmoid
        mixed[at_rows, :] = (silu * upward).astype(BF16)
        grad_gu[at_rows, :piece] = (upward * sigmoid * (1.0 + gate * (1.0 - sigmoid))).astype(BF16)
        grad_gu[at_rows, piece:] = silu.astype(BF16)
        return unused

    lax.fori_loop(0, 8, feed, 0)
    tall_own[...] = tn(mixed[...], cot_all[...]).astype(BF16).reshape(tall_own.shape)
    done = chain_steps(0, SHARE[0])

    def feed_back(number, unused):
        core = jnp.where(number < 2, 1 - place.core, place.core)
        at_rows = pl.ds(pl.multiple_of((number % 2 * 2 + core) * rows, 16), rows)
        grad_mixed = nt(cot_all[at_rows, :], down_piece[...])
        grad_gate = (grad_mixed * grad_gu[at_rows, :piece].astype(F32)).astype(BF16)
        grad_upward = (grad_mixed * grad_gu[at_rows, piece:].astype(F32)).astype(BF16)
        grad_gu[at_rows, :piece] = grad_gate
        grad_gu[at_rows, piece:] = grad_upward
        grad_part[at_rows, :] = (
            nt(grad_gate, gate_piece[...]) + nt(grad_upward, up_piece[...])
        ).astype(BF16)
        mlp_part[at_rows, :] = nn(mixed[at_rows, :], down_piece[...]).astype(BF16)
        chain_step(number + SHARE[0])
        return unused

    done += 4
    lax.fori_loop(0, 2, feed_back, 0)
    grad_sum.start()
    lax.fori_loop(2, 4, feed_back, 0)
    grad_sum.after_core()
    grad_sum.cross()
    both = tn(normed_all[...], grad_gu[...])
    count = wide_own.shape[0] // 2
    for number in range(2):
        wide_own[number * count : (number + 1) * count] = (
            both[:, number * piece : (number + 1) * piece]
            .astype(BF16)
            .reshape(count, *wide_own.shape[1:])
        )
    gather.finish(True)

    qt[...] = qt_in[...]
    at = HEAD_DIM + slots
    qt[at : at + 16, :] = split_rows(-lse[...], 0, 16)
    natural_q = jnp.transpose(qt_in[0:HEAD_DIM, :].astype(F32)).astype(BF16)
    q_pad[...] = jnp.concatenate([natural_q, jnp.zeros_like(natural_q)], axis=1)

    mlp_sum.start()
    done = chain_steps(done, SHARE[1])
    grad_sum.after_cross()
    done = chain_steps(done, SHARE[2])

    normed = resid * factor
    grad_normed = grad_sum.result()
    gains[:, features:] = jnp.sum(grad_normed * normed, axis=0, keepdims=True)
    weighted = grad_normed * gain[...]
    inner = jnp.mean(weighted * normed, axis=-1, keepdims=True)
    grad_resid = cot[my_rows, :].astype(F32) + factor * (weighted - normed * inner)
    resid_grad[...] = grad_resid
    branch[my_rows, :] = grad_resid.astype(BF16)
    send(
        branch.at[my_rows],
        branch.at[my_rows],
        pair_sems.at[0],
        pair_sems.at[1],
        place.partner,
    )
    mlp_sum.after_core()
    mlp_sum.cross()
    done = chain_steps(done, SHARE[3])
    arrived(branch.at[other_rows], pair_sems.at[1], place.partner)

    grads = branch[...]
    outs_part = sum_o[0]
    outs_part[...] = tn(att[...], grads).astype(BF16).reshape(outs_part.shape)
    outs_quad.start()
    grad_att = nt(grads, out_weight[...]).astype(BF16)
    half_width = queries // 2
    filler = jnp.zeros((half_width - heads * half, HEAD_DIM), BF16)
    stacked = jnp.concatenate(
        [
            part
            for number in range(2)
            for part in (
                *(
                    grad_att[
                        number * half : (number + 1) * half,
                        head * HEAD_DIM : (head + 1) * HEAD_DIM,
                    ]
                    for head in range(heads)
                ),
                filler,
            )
        ],
        axis=0,
    )
    do_pad[...] = jnp.concatenate([jnp.zeros_like(stacked), stacked], axis=1)
    turned = jnp.transpose(stacked.astype(F32))
    delta = jnp.sum(turned * ot[...], axis=0, keepdims=True)
    dot_t[0:HEAD_DIM, :] = split_rows(-delta, 0, HEAD_DIM)
    dot_t[HEAD_DIM:, :] = turned.astype(BF16)
    done = chain_steps(done, SHARE[4])
    outs_quad.middle()

    def write_layer():
        layer_out[my_rows, :] = (resid_in[...] + mlp_sum.result()).astype(BF16)
        send(
            layer_out.at[my_rows],
            layer_out.at[my_rows],
            pair_sems.at[2],
            pair_sems.at[3],
            place.partner,
        )

    dq_out[...] = jnp.zeros_like(dq_out)

    def chunk_place(number):
        far = 1 - number % 2
        group = (place.group + 1 + number // 2) % groups
        side = place.side + far * (1 - 2 * place.side)
        return group, side

    lane = lax.broadcasted_iota(jnp.int32, (1, LANES), 1)
    ones = jnp.where(lane < 3, 1.0, 0.0).astype(BF16)

    def attend_back(number, slot, own_chip=False):
        group, side = chunk_place(number)
        chip = group * 2 + side
        at_rows = pl.ds(pl.multiple_of(chip * span, 16), span)
        kv = kv_all[at_rows, :]
        keys = extended_keys(kv, chip, rows, width, slots)
        values = jnp.where(lane >= HEAD_DIM, kv, jnp.broadcast_to(ones, kv.shape))
        for part in range(parts):
            lanes = slice(part * block, (part + 1) * block)
            score = nn(keys, qt[:, lanes])
            if own_chip:
                first = part * block
                number_of_half = first // half_width
                score = hide_later(score, place, rows, number_of_half, first % half_width)
            weights = jnp.exp(score)
            change = nn(values, dot_t[:, lanes])
            low = (weights * change).astype(BF16)
            total = nn(weights.astype(BF16), do_pad[lanes, :]) + nn(low, q_pad[lanes, :])
            if part == 0:
                dkv[slot] = total
            else:
                dkv[slot] += total
            dq_out[:, lanes] += tn(kv[:, :HEAD_DIM], low)

    def hand_over(number, slot):
        other = pl.ds(pl.multiple_of((1 - place.core) * rows, 16), rows)

        @pl.when(number >= 2)
        def free_again():
            sent(sib_send.at[slot], kv_sems.at[0, number - 2], place.sibling)

        sib_send[slot] = dkv[slot, other, :].astype(BF16)
        send(
            sib_send.at[slot],
            sib_in.at[number],
            kv_sems.at[0, number],
            kv_sems.at[1, number],
            place.sibling,
        )

    def take_over(number, near, own_group=False):
        group, side = chunk_place(number)
        step = number // 2
        arrived(sib_in.at[number], kv_sems.at[1, number], place.sibling)
        mine = pl.ds(pl.multiple_of(place.core * rows, 16), rows)
        total = dkv[1 if near else 0, mine, :] + sib_in[number].astype(F32)
        if not near:
            ring = step % 2

            @pl.when(step >= 2)
            def side_free():
                sent(side_send.at[0], kv_sems.at[2, step - 2], place.across)

            side_send[ring] = total.astype(BF16)
            send(
                side_send.at[ring],
                side_in.at[step],
                kv_sems.at[2, step],
                kv_sems.at[3, step],
                place.across,
            )
            return
        arrived(side_in.at[step], kv_sems.at[3, step], place.across)
        total = total + side_in[step].astype(F32)
        if own_group:
            dkv_out[...] = total
            return
        ring = step % 2

        @pl.when(step >= 2)
        def column_free():
            sent(z_send.at[0], kv_sems.at[4, step - 2], place.sibling)

        z_send[ring] = total.astype(BF16)
        back = groups - 2 - step
        send(
            z_send.at[ring],
            z_in.at[back],
            kv_sems.at[4, step],
            kv_sems.at[5, back],
            place.in_group(group),
        )

    each = 1

    def pair(step, unused):
        attend_back(2 * step, 0)
        hand_over(2 * step, 0)
        chain_steps(done + 2 * each * step, each)

        @pl.when(step > 0)
        def last_near():
            take_over(2 * step - 1, True)

        attend_back(2 * step + 1, 1)
        hand_over(2 * step + 1, 1)
        take_over(2 * step, False)
        chain_steps(done + 2 * each * step + each, each)

        @pl.when(step == 0)
        def outs_ready():
            mlp_sum.after_cross()
            outs_quad.end()
            outs_sum.start()

        @pl.when(step == 1)
        def layer_ready():
            write_layer()
            outs_sum.middle()

        return unused

    lax.fori_loop(0, groups - 1, pair, 0)
    outs_sum.end()
    done += 2 * each * (groups - 1)
    attend_back(chunks - 2, 0)
    hand_over(chunks - 2, 0)
    done = chain_steps(done, each)
    if groups > 1:
        take_over(chunks - 3, True)
    attend_back(chunks - 1, 1, True)
    hand_over(chunks - 1, 1)
    take_over(chunks - 2, False)
    done = chain_steps(done, SHARE[5])

    quarter = HEAD_DIM // 2
    raw = dq_out[...] * HEAD_DIM**-0.5
    one, two = raw[:quarter, :], raw[quarter:, :]
    cos, sin = turns[:quarter, :], turns[quarter:, :]
    turned = jnp.concatenate([one * cos + two * sin, two * cos - one * sin], axis=0)
    natural = jnp.transpose(turned).astype(BF16)
    grad_query = jnp.concatenate(
        [
            jnp.concatenate(
                [
                    natural[start + head * half : start + (head + 1) * half, :]
                    for head in range(heads)
                ],
                axis=1,
            )
            for start in (0, half_width)
        ],
        axis=0,
    )
    x_all = x_in[...].astype(F32)
    factor_all = lax.rsqrt(jnp.mean(x_all * x_all, axis=-1, keepdims=True) + EPSILON)
    normed_attn = (x_all * factor_all * attn_gain[...]).astype(BF16)
    wide_q = grad_query.shape[1]
    q_part = sum_q[0]
    q_part[...] = tn(grad_query, normed_attn).astype(BF16).reshape(q_part.shape)
    q_quad.start()
    turn_send[...] = nn(grad_query, weights_in[:wide_q, :])
    biases[...] = jnp.zeros_like(biases)
    biases[:, :wide_q] = jnp.sum(grad_query.astype(F32), axis=0, keepdims=True)
    done = chain_steps(done, SHARE[11])
    take_over(chunks - 1, True, True)
    q_quad.middle()
    outs_sum.cross()
    done = chain_steps(done, SHARE[6])
    for step in range(groups - 1):
        arrived(z_in.at[step], kv_sems.at[5, step], place.sibling)
        dkv_out[...] += z_in[step].astype(F32)
    turned = jnp.transpose(dkv_out[...])
    one, two = turned[:quarter, :], turned[quarter:HEAD_DIM, :]
    cos, sin = turns_rows[:quarter, :], turns_rows[quarter:, :]
    turned = jnp.concatenate(
        [one * cos + two * sin, two * cos - one * sin, turned[HEAD_DIM:, :]], axis=0
    )
    grad_kv = jnp.transpose(turned).astype(BF16)
    kv_part = sum_kv[0]
    kv_part[...] = tn(grad_kv, normed_attn).astype(BF16).reshape(kv_part.shape)
    kv_quad.start()
    turn_send[...] += nn(grad_kv, weights_in[wide_q:, :])
    turn_in[0] = turn_send[other_rows, :].astype(BF16)
    send(turn_in.at[0], turn_in.at[1], vector_sems.at[0], vector_sems.at[1], place.partner)
    biases[:, wide_q : wide_q + LANES] = jnp.sum(grad_kv.astype(F32), axis=0, keepdims=True)
    done = chain_steps(done, SHARE[12])
    kv_quad.middle()
    q_quad.end()
    q_sum.start()
    done = chain_steps(done, SHARE[7])
    kv_quad.end()
    kv_sum.start()
    x_half = x_in[my_rows, :].astype(F32)
    factor = lax.rsqrt(jnp.mean(x_half * x_half, axis=-1, keepdims=True) + EPSILON)
    normed = x_half * factor
    done = chain_steps(done, SHARE[13])
    arrived(turn_in.at[1], vector_sems.at[1], place.partner)
    grad_normed = turn_send[my_rows, :] + turn_in[1].astype(F32)
    gains[:, :features] = jnp.sum(grad_normed * normed, axis=0, keepdims=True)
    weighted = grad_normed * attn_gain[...]
    mean = jnp.mean(weighted * normed, axis=-1, keepdims=True)
    input_grad[my_rows, :] = (
        resid_grad[...] + factor * (weighted - normed * mean)
    ).astype(BF16)

    def vectors(hop, device, with_biases):
        send(gains, gain_in.at[hop], vector_sems.at[4 + 4 * hop], vector_sems.at[5 + 4 * hop], device)
        if with_biases:
            send(
                biases,
                bias_in.at[hop],
                vector_sems.at[6 + 4 * hop],
                vector_sems.at[7 + 4 * hop],
                device,
            )

    def vectors_done(hop, device, with_biases):
        arrived(gain_in.at[hop], vector_sems.at[5 + 4 * hop], device)
        sent(gains, vector_sems.at[4 + 4 * hop], device)
        gains[...] += gain_in[hop]
        if with_biases:
            arrived(bias_in.at[hop], vector_sems.at[7 + 4 * hop], device)
            sent(biases, vector_sems.at[6 + 4 * hop], device)
            biases[...] += bias_in[hop]

    hops = ((place.partner, False), (place.sibling, True), (place.across, True))
    vectors(0, *hops[0])
    send(
        input_grad.at[my_rows],
        input_grad.at[my_rows],
        vector_sems.at[2],
        vector_sems.at[3],
        place.partner,
    )
    done = chain_steps(done, SHARE[14])
    q_sum.middle()
    vectors_done(0, *hops[0])
    vectors(1, *hops[1])
    kv_sum.middle()
    done = chain_steps(done, SHARE[8])
    vectors_done(1, *hops[1])
    vectors(2, *hops[2])
    done = chain_steps(done, SHARE[9])
    vectors_done(2, *hops[2])
    gain_z[place.group] = gains[...]
    bias_z[place.group] = biases[...]
    base = 16
    for step in range(1, groups):
        other = place.in_group((place.group + step) % groups)
        for number, ref in enumerate((gain_z, bias_z)):
            send(
                ref.at[place.group],
                ref.at[place.group],
                vector_sems.at[base + 4 * step + 2 * number],
                vector_sems.at[base + 4 * (groups - step) + 2 * number + 1],
                other,
            )
    q_sum.end()
    kv_sum.end()
    done = chain_steps(done, SHARE[10])
    q_sum.cross()
    kv_sum.cross()
    for step in range(1, groups):
        other = (place.group + groups - step) % groups
        for number, ref in enumerate((gain_z, bias_z)):
            arrived(
                ref.at[other],
                vector_sems.at[base + 4 * (groups - step) + 2 * number + 1],
                place.sibling,
            )
            sent(
                ref.at[place.group],
                vector_sems.at[base + 4 * step + 2 * number],
                place.sibling,
            )
    gains[...] = jnp.sum(gain_z[...], axis=0)
    biases[...] = jnp.sum(bias_z[...], axis=0)

    def last(number, unused):
        chain_step(number)
        return unused

    lax.fori_loop(done, all_steps, last, 0)

    arrived(input_grad.at[other_rows], vector_sems.at[3], place.partner)
    sent(input_grad.at[my_rows], vector_sems.at[2], place.partner)
    sent(turn_in.at[0], vector_sems.at[0], place.partner)
    for part in (outs_quad, q_quad, kv_quad, outs_sum, q_sum, kv_sum):
        part.finish()
    arrived(layer_out.at[other_rows], pair_sems.at[3], place.partner)
    sent(branch.at[my_rows], pair_sems.at[0], place.partner)
    sent(branch.at[my_rows], pair_sems.at[2], place.partner)
    grad_sum.finish()
    mlp_sum.finish()
    tall_sum.finish()
    wide_sum.finish()
    for number in range(chunks - 2, chunks):
        sent(sib_send.at[0], kv_sems.at[0, number], place.sibling)
    for step in range(groups - 2, groups):
        sent(side_send.at[0], kv_sems.at[2, step], place.across)
    for step in range(groups - 3, groups - 1):
        sent(z_send.at[0], kv_sems.at[4, step], place.sibling)


def vmem_specs(count):
    return [pl.BlockSpec(memory_space=pltpu.VMEM)] * count


def params(collective):
    return pltpu.CompilerParams(
        collective_id=collective, has_side_effects=True, vmem_limit_bytes=VMEM_LIMIT
    )


def attend(groups, slots, kv_own, qt, x_in, out_weight, cot):
    rows, features = x_in.shape
    half = rows // 2
    total = groups * QUAD * rows
    width, queries = qt.shape
    dma = pltpu.SemaphoreType.DMA
    shape = jax.ShapeDtypeStruct
    return pl.pallas_call(
        functools.partial(attend_kernel, groups, slots),
        out_shape=[
            shape((total, LANES), BF16),
            shape((QUAD * rows, features), BF16),
            shape((half, features), F32),
            shape((rows, out_weight.shape[0]), BF16),
            shape((HEAD_DIM, queries), F32),
            shape((1, queries), F32),
        ],
        in_specs=vmem_specs(5),
        out_specs=vmem_specs(6),
        scratch_shapes=[
            pltpu.VMEM((2, 2 * rows, queries // 2), F32),
            pltpu.VMEM((1, queries), F32),
            pltpu.VMEM((1, queries), F32),
            pltpu.VMEM((half, features), BF16),
            pltpu.VMEM((half, features), BF16),
            dma((groups * QUAD,)),
            dma((groups,)),
            dma((groups,)),
            dma((2 * groups,)),
            dma((8,)),
            dma((2,)),
            dma((8,)),
            dma((2,)),
        ],
        compiler_params=params(1),
        name="attend",
    )(kv_own, qt, x_in, out_weight, cot)


def backward(groups, slots, operands):
    (gate_weight, _, _, cot_all, resid, cot, gain, out_weight, att, ot, lse, qt, kv_all) = operands[
        :13
    ]
    weights_in = operands[15]
    rows, inner = att.shape
    half = rows // 2
    features, hidden = gate_weight.shape
    piece = piece_width(hidden)
    layer_rows = QUAD * rows
    width, queries = qt.shape
    chunks = 2 * groups
    both = round_up(weights_in.shape[0], LANES)
    dma = pltpu.SemaphoreType.DMA
    shape = jax.ShapeDtypeStruct
    pass_shape = (rows, LANES)
    wide = jax.ShapeDtypeStruct((2 * features // WIDE_ROWS, WIDE_ROWS, piece), BF16)
    tall = jax.ShapeDtypeStruct((piece // TALL_ROWS, TALL_ROWS, features), BF16)
    outs = (inner // QUAD, features)
    ins_q = (inner // QUAD, features)
    ins_kv = (LANES // QUAD, features)
    return pl.pallas_call(
        functools.partial(backward_kernel, groups, slots),
        out_shape=[
            shape((rows, features), BF16),
            shape((rows, features), BF16),
            shape((QUAD, *wide.shape), BF16),
            shape((QUAD, *tall.shape), BF16),
            *(shape((QUAD, *column_parts(groups, *dims)), BF16) for dims in (outs, ins_q, ins_kv)),
            shape((1, 2 * features), F32),
            shape((1, both), F32),
        ],
        in_specs=[pl.BlockSpec(memory_space=pl.ANY)] * 3 + vmem_specs(15),
        out_specs=vmem_specs(2) + [pl.BlockSpec(memory_space=pl.ANY)] * 5 + vmem_specs(2),
        scratch_shapes=[
            pltpu.VMEM(wide.shape, BF16),
            pltpu.VMEM(tall.shape, BF16),
            pltpu.VMEM(wide.shape, BF16),
            pltpu.VMEM(tall.shape, BF16),
            pltpu.VMEM((round_up(wide.shape[0], 2) // 2, *wide.shape[1:]), BF16),
            pltpu.VMEM((round_up(tall.shape[0], 2) // 2, *tall.shape[1:]), BF16),
            *chain_sems(wide.shape[0]),
            *chain_sems(tall.shape[0]),
            *layer_sum_scratch(half, features),
            *layer_sum_scratch(half, features),
            pltpu.VMEM((rows, features), BF16),
            pltpu.VMEM((width, queries), BF16),
            pltpu.VMEM((LANES, queries), BF16),
            pltpu.VMEM((queries, LANES), BF16),
            pltpu.VMEM((queries, LANES), BF16),
            pltpu.VMEM((2, 2 * rows, LANES), F32),
            pltpu.VMEM((2, *pass_shape), BF16),
            pltpu.VMEM((chunks, *pass_shape), BF16),
            pltpu.VMEM((2, *pass_shape), BF16),
            pltpu.VMEM((groups, *pass_shape), BF16),
            pltpu.VMEM((2, *pass_shape), BF16),
            pltpu.VMEM((groups, *pass_shape), BF16),
            dma((6, chunks)),
            dma((7,)),
            pltpu.VMEM((HEAD_DIM, queries), F32),
            pltpu.VMEM((rows, LANES), F32),
            pltpu.VMEM((half, features), F32),
            pltpu.VMEM((rows, features), F32),
            pltpu.VMEM((2, half, features), BF16),
            pltpu.VMEM((3, 1, 2 * features), F32),
            pltpu.VMEM((3, 1, both), F32),
            pltpu.VMEM((groups, 1, 2 * features), F32),
            pltpu.VMEM((groups, 1, both), F32),
            dma((16 + 4 * groups + 4,)),
            *column_sum_scratch(groups, *outs),
            *column_sum_scratch(groups, *ins_q),
            *column_sum_scratch(groups, *ins_kv),
            pltpu.VMEM((features, piece), BF16),
            pltpu.VMEM((features, piece), BF16),
            pltpu.VMEM((piece, features), BF16),
            pltpu.VMEM((layer_rows, features), BF16),
            pltpu.VMEM((layer_rows, piece), BF16),
            pltpu.VMEM((layer_rows, 2 * piece), BF16),
            pltpu.VMEM((layer_rows, features), BF16),
            pltpu.VMEM((layer_rows, features), BF16),
            dma((8,)),
            dma((2,)),
            dma((8,)),
        ],
        compiler_params=params(2),
        name="backward",
    )(*operands)


def rope_tables(positions, head_size):
    half_size = head_size // 2
    exponent = jnp.arange(half_size, dtype=F32) * (2.0 / head_size)
    frequency = jnp.power(ROPE_BASE, -exponent)
    angle = positions.astype(F32)[:, None] * frequency[None, :]
    return (jnp.cos(angle)[:, None, :], jnp.sin(angle)[:, None, :])


def rotate(values, cosine, sine):
    half_size = values.shape[-1] // 2
    first = values[..., :half_size]
    second = values[..., half_size:]
    return jnp.concatenate(
        [first * cosine - second * sine, second * cosine + first * sine], axis=-1
    )


def piece_width(hidden):
    return round_up(hidden // LANES, QUAD) // QUAD * LANES


def per_device(
    groups,
    layer_input,
    block_order,
    attn_gain,
    query_weight,
    query_bias,
    key_weight,
    key_bias,
    value_weight,
    value_bias,
    out_weight,
    mlp_gain,
    gate_weight,
    up_weight,
    down_weight,
    out_cotangent,
):
    rows, features = layer_input.shape
    block_rows = rows // 2
    slots = block_order.shape[0]
    hidden = gate_weight.shape[1]
    heads = query_weight.shape[1] // HEAD_DIM
    piece = piece_width(hidden)
    half_width = round_up(heads * block_rows, 2 * LANES)
    queries = 2 * half_width
    width = round_up(HEAD_DIM + slots + 16, LANES)
    scale = HEAD_DIM ** (-0.5)
    seq_index = lax.axis_index("seq")
    own_slots = lax.dynamic_slice_in_dim(block_order, 2 * seq_index, 2)
    steps_in = jnp.arange(block_rows, dtype=jnp.int32)
    own_places = (own_slots[:, None] * block_rows + steps_in[None, :]).reshape(-1)
    cosine, sine = rope_tables(own_places, HEAD_DIM)
    inputs = layer_input.astype(F32)
    factor_first = lax.rsqrt(jnp.mean(inputs * inputs, axis=-1, keepdims=True) + EPSILON)
    normed_first = inputs * factor_first
    normed_attn = (normed_first * attn_gain).astype(BF16)
    query_rows = (
        jnp.dot(normed_attn, query_weight, preferred_element_type=F32) + query_bias
    ).reshape(rows, heads, HEAD_DIM)
    key_rows = (jnp.dot(normed_attn, key_weight, preferred_element_type=F32) + key_bias).reshape(
        rows, 1, HEAD_DIM
    )
    value_rows = (
        jnp.dot(normed_attn, value_weight, preferred_element_type=F32) + value_bias
    ).astype(BF16)
    query_rot = rotate(query_rows, cosine, sine).astype(BF16)
    key_rot = rotate(key_rows, cosine, sine).astype(BF16).reshape(rows, HEAD_DIM)
    kv_own = jnp.concatenate([key_rot, value_rows], axis=1)
    padding = ((0, 0), (0, 0), (0, half_width - heads * block_rows))

    def by_columns(values):
        count = values.shape[-1]
        values = values.reshape(2, block_rows, heads, count)
        values = jnp.transpose(values, (3, 0, 2, 1)).reshape(count, 2, heads * block_rows)
        return jnp.pad(values, padding).reshape(count, queries)

    query_t = by_columns(query_rot * jnp.asarray(scale, BF16))
    later = block_order[:, None] > own_slots[None, :]
    bias = jnp.where(later, NEGATIVE, 0.0).astype(BF16)
    bias = jnp.broadcast_to(bias[:, :, None], (slots, 2, half_width)).reshape(slots, queries)
    qt = jnp.concatenate(
        [query_t, bias, jnp.zeros((width - HEAD_DIM - slots, queries), BF16)], axis=0
    )
    gain_row = mlp_gain[None, :]

    kv_all, cot_all, resid, att, ot, lse = attend(
        groups, slots, kv_own, qt, layer_input, out_weight, out_cotangent
    )

    weights_in = jnp.concatenate(
        [jnp.transpose(w) for w in (query_weight, key_weight, value_weight)], axis=0
    )
    turns_rows = jnp.concatenate([cosine[:, 0, :], sine[:, 0, :]], axis=1)
    tables = (
        by_columns(jnp.broadcast_to(turns_rows[:, None, :], (rows, heads, HEAD_DIM))),
        jnp.transpose(turns_rows),
    )
    layer_output, input_grad, wide_sum, tall_sum, outs, ins_q, ins_kv, gains, biases = backward(
        groups,
        slots,
        (
            gate_weight, up_weight, down_weight, cot_all, resid, out_cotangent, gain_row, out_weight,
            att, ot, lse, qt, kv_all, layer_input, attn_gain[None, :], weights_in, *tables,
        ),
    )

    keep = hidden - (QUAD - 1) * piece
    wide_sum = wide_sum.reshape(QUAD, 2, features, piece)
    tall_sum = tall_sum.reshape(QUAD, piece, features)

    def side_by_side(number):
        parts = [wide_sum[i, number] for i in range(QUAD - 1)] + [
            wide_sum[QUAD - 1, number][:, :keep]
        ]
        return jnp.concatenate(parts, axis=1).astype(F32)

    gate_sum, up_sum = side_by_side(0), side_by_side(1)
    down_sum = tall_sum.reshape(QUAD * piece, features)[:hidden].astype(F32)

    query_width = heads * HEAD_DIM

    def quarters(parts, row_count):
        parts = parts.reshape(QUAD, -1, parts.shape[-1])[:, : row_count // QUAD]
        return parts.reshape(row_count, -1).astype(F32)

    out_grad = quarters(outs, query_width)
    query_grad = jnp.transpose(quarters(ins_q, query_width))
    key_value = quarters(ins_kv, 2 * HEAD_DIM)
    key_grad = jnp.transpose(key_value[:HEAD_DIM])
    value_grad = jnp.transpose(key_value[HEAD_DIM:])
    attn_gain_grad, mlp_gain_grad = gains[0, :features], gains[0, features:]
    query_bias_grad = biases[0, :query_width]
    key_bias_grad = biases[0, query_width : query_width + HEAD_DIM]
    value_bias_grad = biases[0, query_width + HEAD_DIM : query_width + 2 * HEAD_DIM]
    return (
        layer_output,
        input_grad,
        attn_gain_grad,
        query_grad,
        query_bias_grad,
        key_grad,
        key_bias_grad,
        value_grad,
        value_bias_grad,
        out_grad,
        mlp_gain_grad,
        gate_sum,
        up_sum,
        down_sum,
    )


def solution(mesh):
    groups = mesh.shape["seq"] // QUAD
    by_rows, columns, rows, vector, whole = (
        P("seq", None),
        P(None, "tp"),
        P("tp", None),
        P("tp"),
        P(),
    )
    return jax.shard_map(
        functools.partial(per_device, groups),
        mesh=mesh,
        in_specs=(
            by_rows, whole, whole, columns, vector, columns, vector, columns, vector, rows,
            whole, columns, columns, rows, by_rows,
        ),
        out_specs=(
            by_rows, by_rows, whole, columns, vector, columns, vector, columns, vector, rows,
            whole, columns, columns, rows,
        ),
        check_vma=False,
    )
```

profile of v0, /device:TPU:0, one launch (start us, length us, event | category | flops | bytes accessed | tf_op | source)
XLA Modules:
  0.0 245.6 jit_solution(9690615734347059729)
XLA Ops:
  0.6 0.7 broadcast_multiply_fusion
  1.8 1.2 fusion.2
  3.1 1.8 convolution_add_fusion
  6.0 0.4 reshape.271
  7.4 0.9 maximum_maximum_fusion.qt.qt_in
  8.7 0.6 fusion.15
  9.8 0.7 pad_maximum_fusion.2.kv_own
  10.5 40.5 %attend.1 = (bf16[4608,128]{1,0:T(8,128)(2,1)}, bf16[1152,896]{1,0:T(8,128)(2,1)}, f32[144,896]{1,0:T(8,128)}, bf16[288,448]{1,0:T(8,128)(2,1)}, f32[64,2048]{1,0:T(8,128)}, /*index=5*/f32[1,2048]{1,0:T(1,128)}) custom-call(bf16[288,128]{1,0:T(8,128)(2,1)} %pad_maximum_fusion.2.kv_own, bf16[128,2048]{1,0:T(8,128)(2,1)} %maximum_maximum_fusion.qt.qt_in, ...), custom_call_target="tpu_custom_call" | custom-call | tf_op jit(solution)/shard_map/attend/pallas_call | solution.py:1495
  51.0 0.6 maximum_bitcast_fusion.turns_rows
  53.1 1.0 copy.56
  54.0 1.0 pad_maximum_fusion.weights_in
  55.1 0.6 broadcast_in_dim.22.gain
  55.7 0.6 broadcast_in_dim.23.attn_gain
  56.2 167.5 %backward.1 = (bf16[288,896]{1,0:T(8,128)(2,1)}, bf16[288,896]{1,0:T(8,128)(2,1)}, bf16[4,14,128,640]{3,2,1,0:T(8,128)(2,1)}, bf16[4,10,64,896]{3,2,1,0:T(8,128)...) custom-call(bf16[896,2432]{1,0:T(8,128)(2,1)} %gate_weight.1, ...), custom_call_target="tpu_custom_call" | custom-call | tf_op jit(solution)/shard_map/backward/pallas_call | solution.py:1548
  223.8 4.1 %slice_bitcast_fusion.3 = (bf16[896,640]{1,0:T(8,128)(2,1)S(1)}, bf16[896,640]{1,0:T(8,128)(2,1)S(1)}, bf16[896,640]{1,0:T(8,128)(2,1)S(1)}, bf16[896,640]{1,0:T...) fusion(bf16[4,2,896,640]{3,2,1,0:T(8,128)(2,1)} %bitcast.73), kind=kLoop, calls=%fused_computation.10 | loop fusion | bytes 18350080 | tf_op jit(solution)/shard_map/squeeze | solution.py:1729
  228.0 6.9 %maximum_convert_fusion = (f32[896,2432]{1,0:T(8,128)}, f32[896,2432]{1,0:T(8,128)}) fusion(bf16[896,512]{1,0:T(8,128)(2,1)S(1)} %slice.121, bf16[896,640]{1,0:T(8,128)(2,1)S(1)} %get-tuple-element.53, bf16[896,640]{1,0:T(8,128)(2,1)S(1)} %get-tuple-element.54, bf16[896,640]{1,0:T(8,128)(2,1)S(1)} %get-tuple-element.55, bf16[896,512]{1,0:T(8,128)(2,1)S(1)} %slice.126, ...), kind=kLoop, calls=%fused_computation.1 | loop fusion | flops 34865152 | bytes 26148864 | tf_op jit(solution)/shard_map/convert_element_type | solution.py:1732
  234.9 4.1 %slice_convert_fusion = f32[2432,896]{1,0:T(8,128)} fusion(bf16[2560,896]{1,0:T(8,128)(2,1)S(1)} %bitcast.76), kind=kLoop, calls=%fused_computation | loop fusion | flops 2179072 | bytes 13074432 | tf_op jit(solution)/shard_map/convert_element_type | solution.py:1735
  239.2 2.0 convert_bitcast_fusion
  241.2 0.8 fusion.19
  242.0 0.6 slice_reduce_fusion
  242.7 0.6 slice.87
  243.2 0.6 slice_bitcast_fusion.8
  243.8 0.8 copy.59
  244.6 0.8 copy.60
  (70 shorter events, 4.7 us)
Async XLA Ops:
  4.9 2.1 copy-start.13
  4.9 3.4 %copy-start = (bf16[288,896]{1,0:T(8,128)(2,1)S(1)}, bf16[288,896]{1,0:T(8,128)(2,1)}, u32[]{:S(2)}) copy-start(bf16[288,896]{1,0:T(8,128)(2,1)} %x_in.3) | copy-start | bytes 1548292
  4.9 3.4 %copy-start.8 = (bf16[896,64]{0,1:T(8,128)(2,1)S(1)}, bf16[896,64]{0,1:T(8,128)(2,1)}, u32[]{:S(2)}) copy-start(bf16[896,64]{0,1:T(8,128)(2,1)} %param.20) | copy-start | bytes 344068
  4.9 3.4 %copy-start.11 = (f32[896]{0:T(1024)S(1)}, f32[896]{0:T(1024)}, u32[]{:S(2)}) copy-start(f32[896]{0:T(1024)} %param.17) | copy-start | bytes 10756
  5.0 3.4 %copy-start.14 = (f32[64]{0:T(128)S(1)}, f32[64]{0:T(128)}, u32[]{:S(2)}) copy-start(f32[64]{0:T(128)} %param.21) | copy-start | bytes 772
  5.3 4.1 %copy-start.7 = (bf16[896,64]{0,1:T(8,128)(2,1)S(1)}, bf16[896,64]{0,1:T(8,128)(2,1)}, u32[]{:S(2)}) copy-start(bf16[896,64]{0,1:T(8,128)(2,1)} %param.22) | copy-start | bytes 344068
  5.3 4.0 %copy-start.15 = (f32[64]{0:T(128)S(1)}, f32[64]{0:T(128)}, u32[]{:S(2)}) copy-start(f32[64]{0:T(128)} %param.23) | copy-start | bytes 772
  10.5 43.5 %copy-start.1 = (bf16[896,448]{0,1:T(8,128)(2,1)S(1)}, bf16[896,448]{0,1:T(8,128)(2,1)}, u32[]{:S(2)}) copy-start(bf16[896,448]{0,1:T(8,128)(2,1)} %param.18) | copy-start | bytes 2408452
  51.0 4.0 %copy-start.10 = (f32[896]{0:T(1024)S(1)}, f32[896]{0:T(1024)}, u32[]{:S(2)}) copy-start(f32[896]{0:T(1024)} %param.25) | copy-start | bytes 10756
  227.9 7.0 %slice-start = ((s8[4587520]{0:T(1024)(128)(4,1)}), s8[4194304]{0:T(1024)(128)(4,1)S(1)}, s32[]{:S(2)}) async-start(s8[4587520]{0:T(1024)(128)(4,1)} %bitcast.74), calls=%async_computation | async-start | bytes 8388608
  228.0 6.9 %slice-start.1 = ((s8[4587520]{0:T(1024)(128)(4,1)}), s8[393216]{0:T(1024)(128)(4,1)S(1)}, s32[]{:S(2)}) async-start(s8[4587520]{0:T(1024)(128)(4,1)} %bitcast.74), calls=%async_computation.1 | async-start | bytes 786432
  234.9 4.1 %copy-start.3 = (bf16[4,4,32,896]{3,2,1,0:T(8,128)(2,1)S(1)}, bf16[4,4,32,896]{3,2,1,0:T(8,128)(2,1)}, u32[]{:S(2)}) copy-start(bf16[4,4,32,896]{3,2,1,0:T(8,128)(2,1)} %get-tuple-element.38) | copy-start | bytes 2752516
  234.9 4.2 %copy-start.2 = (bf16[4,4,32,896]{3,2,1,0:T(8,128)(2,1)S(1)}, bf16[4,4,32,896]{3,2,1,0:T(8,128)(2,1)}, u32[]{:S(2)}) copy-start(bf16[4,4,32,896]{3,2,1,0:T(8,128)(2,1)} %get-tuple-element.41) | copy-start | bytes 2752516
  239.0 2.2 copy-start.6
  239.1 3.0 %copy-start.9 = (f32[1,1792]{1,0:T(1,128)S(1)}, f32[1,1792]{1,0:T(1,128)}, u32[]{:S(2)}) copy-start(f32[1,1792]{1,0:T(1,128)} %get-tuple-element.37) | copy-start | bytes 21508
  239.1 3.6 %copy-start.12 = (f32[1,640]{1,0:T(1,128)S(1)}, f32[1,640]{1,0:T(1,128)}, u32[]{:S(2)}) copy-start(f32[1,640]{1,0:T(1,128)} %get-tuple-element.39) | copy-start | bytes 7684
  239.1 4.7 %copy-start.5 = (bf16[288,896]{1,0:T(8,128)(2,1)S(1)}, bf16[288,896]{1,0:T(8,128)(2,1)}, u32[]{:S(2)}) copy-start(bf16[288,896]{1,0:T(8,128)(2,1)} %get-tuple-element.86) | copy-start | bytes 1548292
  239.1 5.5 %copy-start.4 = (bf16[288,896]{1,0:T(8,128)(2,1)S(1)}, bf16[288,896]{1,0:T(8,128)(2,1)}, u32[]{:S(2)}) copy-start(bf16[288,896]{1,0:T(8,128)(2,1)} %get-tuple-element.87) | copy-start | bytes 1548292
where the time goes:
time: 250 us; the launch traced here: 246 us
  Pallas kernels  208 us (83%)
  other arithmetic  20 us (8%)
  local copies, waits for them, and re-layouts  13.8 us (6%)
  matrix products  2.56 us (1%)
    pallas_call x1, Pallas kernels, backward(): pl.pallas_call(functools.partial(backward_kernel, groups, slots), out_sha...  168 us
    pallas_call x1, Pallas kernels, attend(): pl.pallas_call(functools.partial(attend_kernel, groups, slots), out_shape...  40.5 us
    convert_element_type x1, other arithmetic, side_by_side(): return jnp.concatenate(parts, axis=1).astype(F32)  6.88 us

commit v1 on v0

--- a/solution.py
+++ b/solution.py
@@ -1613,6 +1613,33 @@
     )(*operands)
 
 
+def unfold_kernel(keep, gate_in, up_in, gate, up):
+    for src, dst in ((gate_in, gate), (up_in, up)):
+        size = src.shape[2]
+        for number in range(QUAD):
+            count = size if number < QUAD - 1 else keep
+            dst[:, number * size : number * size + count] = src[number, :, :count].astype(F32)
+
+
+def unfold(parts, features, hidden):
+    piece = parts.shape[2]
+    blocks = features // WIDE_ROWS
+    block = (QUAD, WIDE_ROWS, piece)
+    out = pl.BlockSpec((WIDE_ROWS, hidden), lambda i: (i, 0))
+    return pl.pallas_call(
+        functools.partial(unfold_kernel, hidden - (QUAD - 1) * piece),
+        grid=(blocks,),
+        out_shape=[jax.ShapeDtypeStruct((features, hidden), F32)] * 2,
+        in_specs=[
+            pl.BlockSpec(block, lambda i: (0, i, 0)),
+            pl.BlockSpec(block, lambda i: (0, i + blocks, 0)),
+        ],
+        out_specs=[out, out],
+        compiler_params=pltpu.CompilerParams(vmem_limit_bytes=VMEM_LIMIT),
+        name="unfold",
+    )(parts, parts)
+
+
 def rope_tables(positions, head_size):
     half_size = head_size // 2
     exponent = jnp.arange(half_size, dtype=F32) * (2.0 / head_size)
@@ -1721,17 +1748,8 @@
         ),
     )
 
-    keep = hidden - (QUAD - 1) * piece
-    wide_sum = wide_sum.reshape(QUAD, 2, features, piece)
+    gate_sum, up_sum = unfold(wide_sum.reshape(QUAD, 2 * features, piece), features, hidden)
     tall_sum = tall_sum.reshape(QUAD, piece, features)
-
-    def side_by_side(number):
-        parts = [wide_sum[i, number] for i in range(QUAD - 1)] + [
-            wide_sum[QUAD - 1, number][:, :keep]
-        ]
-        return jnp.concatenate(parts, axis=1).astype(F32)
-
-    gate_sum, up_sum = side_by_side(0), side_by_side(1)
     down_sum = tall_sum.reshape(QUAD * piece, features)[:hidden].astype(F32)
 
     query_width = heads * HEAD_DIM

time: 250 us -> 252 us (level)
  Pallas kernels: 208 us -> 218 us
  other arithmetic: 20 us -> 15.5 us
  local copies, waits for them, and re-layouts: 13.8 us -> 9.56 us
    pallas_call x0 -> x1, Pallas kernels: none -> 10.4 us  [unfold(): pl.pallas_call(functools.partial(unfold_kernel, hidden - (QUAD - 1) * pie...]
    convert_element_type x1 -> x0, other arithmetic: 6.88 us -> none  [side_by_side(): return jnp.concatenate(parts, axis=1).astype(F32)]
    squeeze x1 -> x0, local copies, waits for them, and re-layouts: 4.09 us -> none  [side_by_side(): wide_sum[i, number]]
where the time goes in v1:
time: 252 us; the launch traced here: 247 us
  Pallas kernels  218 us (87%)
  other arithmetic  15.5 us (6%)
  local copies, waits for them, and re-layouts  9.56 us (4%)
  matrix products  2.56 us (1%)
    pallas_call x1, Pallas kernels, backward(): pl.pallas_call(functools.partial(backward_kernel, groups, slots), out_sha...  168 us
    pallas_call x1, Pallas kernels, attend(): pl.pallas_call(functools.partial(attend_kernel, groups, slots), out_shape...  40.5 us
    pallas_call x1, Pallas kernels, unfold(): pl.pallas_call(functools.partial(unfold_kernel, hidden - (QUAD - 1) * pie...  10.4 us
    convert_element_type x1, other arithmetic, per_device(): down_sum = tall_sum.reshape(QUAD * piece, features)[:hidden].astype(F32)  6.43 us

profile of v1, /device:TPU:0, one launch (start us, length us, event | category | flops | bytes accessed | tf_op | source)
XLA Modules:
  0.0 247.2 jit_solution(1445859995220303143)
XLA Ops:
  0.6 0.7 broadcast_multiply_fusion
  1.8 1.2 fusion.2
  3.1 1.8 convolution_add_fusion
  6.0 0.4 reshape.271
  7.4 0.9 maximum_maximum_fusion.qt.qt_in
  8.7 0.6 fusion.15
  9.8 0.7 pad_maximum_fusion.2.kv_own
  10.5 40.5 %attend.1 = (bf16[4608,128]{1,0:T(8,128)(2,1)}, bf16[1152,896]{1,0:T(8,128)(2,1)}, f32[144,896]{1,0:T(8,128)}, bf16[288,448]{1,0:T(8,128)(2,1)}, f32[64,2048]{1,0:T(8,128)}, /*index=5*/f32[1,2048]{1,0:T(1,128)}) custom-call(bf16[288,128]{1,0:T(8,128)(2,1)} %pad_maximum_fusion.2.kv_own, bf16[128,2048]{1,0:T(8,128)(2,1)} %maximum_maximum_fusion.qt.qt_in, ...), custom_call_target="tpu_custom_call" | custom-call | tf_op jit(solution)/shard_map/attend/pallas_call | solution.py:1495
  51.1 0.6 maximum_bitcast_fusion.turns_rows
  52.5 0.4 copy.53
  53.1 1.0 copy.56
  54.0 1.0 pad_maximum_fusion.weights_in
  55.1 0.6 broadcast_in_dim.22.gain
  55.7 0.6 broadcast_in_dim.23.attn_gain
  56.2 167.5 %backward.1 = (bf16[288,896]{1,0:T(8,128)(2,1)}, bf16[288,896]{1,0:T(8,128)(2,1)}, bf16[4,14,128,640]{3,2,1,0:T(8,128)(2,1)}, bf16[4,10,64,896]{3,2,1,0:T(8,128)...) custom-call(bf16[896,2432]{1,0:T(8,128)(2,1)} %gate_weight.1, ...), custom_call_target="tpu_custom_call" | custom-call | tf_op jit(solution)/shard_map/backward/pallas_call | solution.py:1548
  223.8 10.4 %unfold.1 = (f32[896,2432]{1,0:T(8,128)}, f32[896,2432]{1,0:T(8,128)}) custom-call(bf16[4,1792,640]{2,1,0:T(8,128)(2,1)} %bitcast.57, bf16[4,1792,640]{2,1,0:T(8,128)(2,1)} %bitcast.58), custom_call_target="tpu_custom_call" | custom-call | tf_op jit(solution)/shard_map/unfold/pallas_call | solution.py:1629
  234.2 6.4 %slice_convert_fusion = f32[2432,896]{1,0:T(8,128)} fusion(bf16[2560,896]{1,0:T(8,128)(2,1)} %bitcast.59), kind=kLoop, calls=%fused_computation | loop fusion | flops 2179072 | bytes 13074432 | tf_op jit(solution)/shard_map/convert_element_type | solution.py:1753
  240.8 2.0 convert_bitcast_fusion
  242.8 0.8 fusion.19
  243.6 0.6 slice_reduce_fusion
  244.3 0.6 slice.57
  244.8 0.6 slice_bitcast_fusion
  245.4 0.8 copy.59
  246.2 0.8 copy.60
  (62 shorter events, 4.2 us)
Async XLA Ops:
  4.9 2.2 copy-start.13
  4.9 3.4 %copy-start = (bf16[288,896]{1,0:T(8,128)(2,1)S(1)}, bf16[288,896]{1,0:T(8,128)(2,1)}, u32[]{:S(2)}) copy-start(bf16[288,896]{1,0:T(8,128)(2,1)} %x_in.3) | copy-start | bytes 1548292
  4.9 3.4 %copy-start.8 = (bf16[896,64]{0,1:T(8,128)(2,1)S(1)}, bf16[896,64]{0,1:T(8,128)(2,1)}, u32[]{:S(2)}) copy-start(bf16[896,64]{0,1:T(8,128)(2,1)} %param.20) | copy-start | bytes 344068
  4.9 3.4 %copy-start.11 = (f32[896]{0:T(1024)S(1)}, f32[896]{0:T(1024)}, u32[]{:S(2)}) copy-start(f32[896]{0:T(1024)} %param.17) | copy-start | bytes 10756
  5.0 3.4 %copy-start.14 = (f32[64]{0:T(128)S(1)}, f32[64]{0:T(128)}, u32[]{:S(2)}) copy-start(f32[64]{0:T(128)} %param.21) | copy-start | bytes 772
  5.3 4.1 %copy-start.7 = (bf16[896,64]{0,1:T(8,128)(2,1)S(1)}, bf16[896,64]{0,1:T(8,128)(2,1)}, u32[]{:S(2)}) copy-start(bf16[896,64]{0,1:T(8,128)(2,1)} %param.22) | copy-start | bytes 344068
  5.3 4.1 %copy-start.15 = (f32[64]{0:T(128)S(1)}, f32[64]{0:T(128)}, u32[]{:S(2)}) copy-start(f32[64]{0:T(128)} %param.23) | copy-start | bytes 772
  10.5 43.5 %copy-start.1 = (bf16[896,448]{0,1:T(8,128)(2,1)S(1)}, bf16[896,448]{0,1:T(8,128)(2,1)}, u32[]{:S(2)}) copy-start(bf16[896,448]{0,1:T(8,128)(2,1)} %param.18) | copy-start | bytes 2408452
  51.0 4.0 %copy-start.10 = (f32[896]{0:T(1024)S(1)}, f32[896]{0:T(1024)}, u32[]{:S(2)}) copy-start(f32[896]{0:T(1024)} %param.25) | copy-start | bytes 10756
  234.2 6.4 %copy-start.3 = (bf16[4,4,32,896]{3,2,1,0:T(8,128)(2,1)S(1)}, bf16[4,4,32,896]{3,2,1,0:T(8,128)(2,1)}, u32[]{:S(2)}) copy-start(bf16[4,4,32,896]{3,2,1,0:T(8,128)(2,1)} %get-tuple-element.40) | copy-start | bytes 2752516
  234.2 6.5 %copy-start.2 = (bf16[4,4,32,896]{3,2,1,0:T(8,128)(2,1)S(1)}, bf16[4,4,32,896]{3,2,1,0:T(8,128)(2,1)}, u32[]{:S(2)}) copy-start(bf16[4,4,32,896]{3,2,1,0:T(8,128)(2,1)} %get-tuple-element.43) | copy-start | bytes 2752516
  240.6 2.2 copy-start.6
  240.7 3.0 %copy-start.9 = (f32[1,1792]{1,0:T(1,128)S(1)}, f32[1,1792]{1,0:T(1,128)}, u32[]{:S(2)}) copy-start(f32[1,1792]{1,0:T(1,128)} %get-tuple-element.39) | copy-start | bytes 21508
  240.7 3.6 %copy-start.12 = (f32[1,640]{1,0:T(1,128)S(1)}, f32[1,640]{1,0:T(1,128)}, u32[]{:S(2)}) copy-start(f32[1,640]{1,0:T(1,128)} %get-tuple-element.41) | copy-start | bytes 7684
  240.7 4.7 %copy-start.5 = (bf16[288,896]{1,0:T(8,128)(2,1)S(1)}, bf16[288,896]{1,0:T(8,128)(2,1)}, u32[]{:S(2)}) copy-start(bf16[288,896]{1,0:T(8,128)(2,1)} %get-tuple-element.80) | copy-start | bytes 1548292
  240.7 5.5 %copy-start.4 = (bf16[288,896]{1,0:T(8,128)(2,1)S(1)}, bf16[288,896]{1,0:T(8,128)(2,1)}, u32[]{:S(2)}) copy-start(bf16[288,896]{1,0:T(8,128)(2,1)} %get-tuple-element.81) | copy-start | bytes 1548292
